TPU v7x, 512 devices: a whole 4x8x8 slice. The times are simulated.
512 devices in a mesh: wide: 32 (over y, x), narrow: 16 (over z, core).
Axes of the slice: x: 4, y: 8, z: 8, core: 2. Of those that a mesh axis runs over, the one named last changes fastest.
Arguments:
- hamiltonian: float32 [1024, 3, 128, 128], P(('wide', 'narrow')), may hold values from -3.3 to 3.3, as said below
- old_density: float32 [1024, 3, 128, 128], P(('wide', 'narrow')), may hold values from -2 to 2
- neighbours: int32 [1024, 3], P(('wide', 'narrow')), may hold values from 0 to 31, as said below
- live: int32 [1024], P(('wide', 'narrow')), may hold values from 0 to 1, as said below
- potential: float32 [1], replicated, may hold values from -1 to 1
Outputs:
- density: float32 [1024, 3, 128, 128], P(('wide', 'narrow'))
Inputs may be any that keep to these rules, and one draw needn't show every extreme that they name: Within each cluster of 32 consecutive blocks, entry 0 is the block's own index in the cluster and entries 1 and 2 are its neighbours on a cycle through all blocks of the cluster: block a is entry 1 of its entry-2 neighbour and entry 2 of its entry-1 neighbour. Along the cycle the 2 blocks of one device stand next to each other in some order; the devices of the narrow axis follow each other in an order drawn from the seed. For each index of the narrow axis, the devices at wide indices i and i + 16 own at most 2 live blocks together; in every draw some device owns 2 live blocks. `hamiltonian`: the block Hamiltonian is symmetric: tile 1 of block c is the transpose of tile 2 of prev(c), and tile 0 is symmetric.
All inputs are finite; a program needn't handle non-finite values. Where the computation divides by a largest or mean magnitude, that divisor is 1e-20 or more.
Results may differ from a plain program's by a relative error of at most 0.0001.
Values sent between devices are 32-bit elements; how exact they have to be, the bound alone decides.
A program may use at most 64 MiB of HBM per device.

v0:
```python
import jax
import jax.numpy as jnp
from jax import lax
from jax.sharding import PartitionSpec as P

ITERS = 4


epsilon = 1e-06


def in_one_piece(arrays, axis, dim, along):
    widths = [a.shape[along] for a in arrays]
    both = jnp.concatenate(arrays, axis=along)
    out = lax.all_gather(both, axis, axis=dim, tiled=True)
    return tuple(jnp.split(out, [sum(widths[:k]) for k in range(1, len(widths))], axis=along))


def product(left, right):
    return jnp.matmul(left, right, precision=lax.Precision.HIGHEST)


def transpose_tiles(tiles):
    return jnp.swapaxes(tiles, -1, -2)


def assemble(row_tiles, prev_onsite, next_onsite, level):
    zero_tile = jnp.zeros_like(prev_onsite)
    upper_rows = jnp.concatenate(
        [row_tiles[..., 0, :, :], row_tiles[..., 1, :, :], row_tiles[..., 2, :, :]], axis=-1
    )
    middle_rows = jnp.concatenate(
        [transpose_tiles(row_tiles[..., 1, :, :]), prev_onsite, zero_tile], axis=-1
    )
    lower_rows = jnp.concatenate(
        [transpose_tiles(row_tiles[..., 2, :, :]), zero_tile, next_onsite], axis=-1
    )
    matrix = jnp.concatenate([upper_rows, middle_rows, lower_rows], axis=-2)
    order = matrix.shape[-1]
    return matrix - level * jnp.eye(order, dtype=jnp.float32)


def sign_columns(matrix, width, depth):
    order = matrix.shape[-1]
    identity = jnp.eye(order, dtype=jnp.float32)
    bound = jnp.max(jnp.sum(jnp.abs(matrix), axis=-1), axis=-1) + epsilon
    current = matrix / bound[..., None, None]
    for sweep in range(depth - 1):
        square = product(current, current)
        current = 0.5 * product(current, 3.0 * identity - square)
    square = product(current, current)
    final_cols = 0.5 * product(current, 3.0 * identity[:, :width] - square[..., :, :width])
    columns = 0.5 * (identity[:, :width] - final_cols)
    return columns.reshape(columns.shape[:-2] + (order // width, width, width))


def shards(hamiltonian, old_density, neighbours, live, potential):
    width = hamiltonian.shape[-1]
    level = potential[0]
    cluster_onsite = lax.all_gather(hamiltonian[:, 0], "narrow", axis=0, tiled=True)
    prev_onsite = jnp.take(cluster_onsite, neighbours[:, 1], axis=0)
    next_onsite = jnp.take(cluster_onsite, neighbours[:, 2], axis=0)
    matrices = assemble(hamiltonian, prev_onsite, next_onsite, level)
    new_cols = sign_columns(matrices, width, ITERS)
    fresh_cols = jnp.where(live[:, None, None, None] == 1, new_cols, old_density)
    prev_side, next_side = in_one_piece((fresh_cols[:, 1], fresh_cols[:, 2]), "narrow", 0, 1)
    from_prev = jnp.take(next_side, neighbours[:, 1], axis=0)
    from_next = jnp.take(prev_side, neighbours[:, 2], axis=0)
    return jnp.stack(
        [
            0.5 * (fresh_cols[:, 0] + transpose_tiles(fresh_cols[:, 0])),
            0.5 * (fresh_cols[:, 1] + transpose_tiles(from_prev)),
            0.5 * (fresh_cols[:, 2] + transpose_tiles(from_next)),
        ],
        axis=1,
    )


def solution(mesh):
    placed = (
        P(("wide", "narrow"), None, None, None),
        P(("wide", "narrow"), None, None, None),
        P(("wide", "narrow"), None),
        P(("wide", "narrow")),
        P(),
    )
    return jax.shard_map(
        shards,
        mesh=mesh,
        in_specs=placed,
        out_specs=P(("wide", "narrow"), None, None, None),
        check_vma=False,
    )
```

profile of v0, /device:TPU:1, one launch (start us, length us, event | category | flops | bytes accessed | tf_op | source)
XLA Modules:
  0.0 140.7 jit_solution(15930580519983071181)
XLA Ops:
  6.5 1.8 %slice_bitcast_fusion.5 = (f32[2,128,128]{2,1,0:T(8,128)S(1)}, f32[2,128,128]{2,1,0:T(8,128)S(1)}, f32[2,128,128]{2,1,0:T(8,128)S(1)}, f32[2,1,128,128]{3,2,1,0:...) fusion(f32[2,3,128,128]{3,2,1,0:T(8,128)} %param.7), kind=kLoop, calls=%fused_computation.51 | loop fusion | bytes 1179648 | tf_op jit(solution)/shard_map/squeeze | solution.py:30
  9.0 0.1 copy.68
  9.1 0.1 copy.69
  9.2 0.2 slice_reduce_fusion.1
  9.7 48.9 %all-gather.6.cloned.1.call-done = f32[32,1,128,128]{3,2,1,0:T(8,128)} async-done(((f32[2,1,128,128]{3,2,1,0:T(8,128)}), f32[32,1,128,128]{3,2,1,0:T(8,128)}) %all-gather.6.cloned.1.call-update) | async-done | bytes 2097168 | tf_op jit(solution)/shard_map/all_gather | solution.py:60
  58.6 2.1 %gather_fusion.1 = f32[2,128,128]{2,1,0:T(8,128)S(1)} fusion(f32[32,128,128]{2,1,0:T(8,128)} %bitcast.68, s32[1024]{0:T(1024)S(1)} %pad_clamp_fusion), kind=kCustom, calls=%fused_computation.1.clone | custom fusion | bytes 262152 | tf_op jit(solution)/shard_map/jit(_take)/gather | solution.py:62
  60.8 2.1 %gather_fusion = f32[2,128,128]{2,1,0:T(8,128)S(1)} fusion(f32[32,128,128]{2,1,0:T(8,128)} %bitcast.69, s32[1024]{0:T(1024)S(1)} %pad_clamp_fusion.1), kind=kCustom, calls=%fused_computation.clone | custom fusion | bytes 262152 | tf_op jit(solution)/shard_map/jit(_take)/gather | solution.py:61
  62.9 0.1 broadcast_select_fusion.1
  63.0 0.1 broadcast_select_fusion
  63.1 0.2 abs_reduce_fusion
  63.3 0.1 reduce_max.9
  63.5 2.6 %convolution_subtract_fusion.2 = f32[2,384,384]{2,1,0:T(8,128)S(1)} fusion(f32[384,384]{1,0:T(8,128)S(1)} %fusion.3, f32[2]{0:T(128)S(1)} %broadcast_add_fusion, f32[2,128,128]{2,1,0:T(8,128)S(1)} %broadcast_select_fusion, f32[2,128,128]{2,1,0:T(8,128)S(1)} %broadcast_in_dim.17, f32[2,128,128]{2,1,0:T(8,128)S(1)} %bitcast.66, ...), kind=kOutput, calls=%fused_computation.9 | convolution fusion | flops 1362198528 | bytes 3407880 | tf_op jit(solution)/shard_map/dot_general | solution.py:20
  66.1 2.5 %convolution_multiply_fusion.2 = f32[2,384,384]{2,1,0:T(8,128)S(1)} fusion(f32[2,384,384]{2,1,0:T(8,128)S(1)} %convolution_subtract_fusion.2, f32[2]{0:T(128)S(1)} %broadcast_add_fusion, f32[2,128,128]{2,1,0:T(8,128)S(1)} %broadcast_select_fusion, f32[2,128,128]{2,1,0:T(8,128)S(1)} %broadcast_in_dim.17, f32[2,128,128]{2,1,0:T(8,128)S(1)} %bitcast.67, ...), kind=kOutput, calls=%fused_computation.8 | convolution fusion | flops 1362198528 | bytes 3997704 | tf_op jit(solution)/shard_map/dot_general | solution.py:20
  68.6 2.5 %convolution_subtract_fusion.1 = f32[2,384,384]{2,1,0:T(8,128)S(1)} fusion(f32[2,384,384]{2,1,0:T(8,128)S(1)} %convolution_multiply_fusion.2, f32[384,384]{1,0:T(8,128)S(1)} %fusion.3), kind=kOutput, calls=%fused_computation.7 | convolution fusion | flops 1359249408 | bytes 2949120 | tf_op jit(solution)/shard_map/dot_general | solution.py:20
  71.1 2.4 %convolution_multiply_fusion.1 = f32[2,384,384]{2,1,0:T(8,128)S(1)} fusion(f32[2,384,384]{2,1,0:T(8,128)S(1)} %convolution_multiply_fusion.2, f32[2,384,384]{2,1,0:T(8,128)S(1)} %convolution_subtract_fusion.1), kind=kOutput, calls=%fused_computation.6 | convolution fusion | flops 1359249408 | bytes 3538944 | tf_op jit(solution)/shard_map/dot_general | solution.py:20
  73.5 2.7 %convolution_subtract_fusion = f32[2,384,384]{2,1,0:T(8,128)S(1)} fusion(f32[2,384,384]{2,1,0:T(8,128)S(1)} %convolution_multiply_fusion.1, f32[384,384]{1,0:T(8,128)S(1)} %fusion.3), kind=kOutput, calls=%fused_computation.5 | convolution fusion | flops 1359249408 | bytes 2949120 | tf_op jit(solution)/shard_map/dot_general | solution.py:20
  76.2 2.4 %convolution_multiply_fusion = f32[2,384,384]{2,1,0:T(8,128)S(1)} fusion(f32[2,384,384]{2,1,0:T(8,128)S(1)} %convolution_multiply_fusion.1, f32[2,384,384]{2,1,0:T(8,128)S(1)} %convolution_subtract_fusion), kind=kOutput, calls=%fused_computation.4 | convolution fusion | flops 1359249408 | bytes 3538944 | tf_op jit(solution)/shard_map/dot_general | solution.py:20
  78.7 1.2 convolution_subtract_fusion.3
  79.9 1.2 fusion.1
  81.1 0.1 copy_select_fusion
  81.2 0.7 pad_maximum_fusion.1
  81.9 0.1 copy.63
  82.0 0.1 copy.62
  82.2 43.7 %all-gather.4.cloned.1.call-done = f32[32,256,128]{2,1,0:T(8,128)} async-done(((f32[2,256,128]{2,1,0:T(8,128)}), f32[32,256,128]{2,1,0:T(8,128)}) %all-gather.4.cloned.1.call-update) | async-done | bytes 4194320 | tf_op jit(solution)/shard_map/all_gather | solution.py:15
  125.9 3.9 %fusion.9 = (f32[32,128,128]{2,1,0:T(8,128)}, f32[32,128,128]{2,1,0:T(8,128)S(1)}) fusion(f32[32,256,128]{2,1,0:T(8,128)} %all-gather.4.cloned.1.call-done), kind=kLoop, calls=%fused_computation.52 | loop fusion | bytes 8388608 | tf_op jit(solution)/shard_map/split | solution.py:16
  129.8 2.1 %gather_fusion.2 = f32[2,128,128]{2,1,0:T(8,128)S(1)} fusion(f32[32,128,128]{2,1,0:T(8,128)} %get-tuple-element.8, s32[1024]{0:T(1024)S(1)} %pad_clamp_fusion.1), kind=kCustom, calls=%fused_computation.2.clone | custom fusion | bytes 262152 | tf_op jit(solution)/shard_map/jit(_take)/gather | solution.py:67
  131.9 0.6 gather_fusion.3
  132.5 0.1 copy.64
  132.6 0.1 bitcast_add_fusion.1
  132.7 0.1 copy.65
  132.8 0.1 fusion.8
  132.9 0.9 copy.66
  (26 shorter events, 0.4 us)
Async XLA Ops:
  6.5 2.7 %copy-start.1 = (s32[2,3]{1,0:T(2,128)S(1)}, s32[2,3]{1,0:T(2,128)}, u32[]{:S(2)}) copy-start(s32[2,3]{1,0:T(2,128)} %param.9) | copy-start | bytes 76
  6.5 52.1 %all-gather.6.cloned.1.call-start = ((), (), s32[]{:S(2)}) async-start(), calls=%async_computation.1 | async-start | bytes 2228224 | tf_op jit(solution)/shard_map/all_gather | solution.py:60
  8.3 1.3 copy-start.2
  8.3 117.5 %all-gather.4.cloned.1.call-start = ((), (), s32[]{:S(2)}) async-start(), calls=%async_computation | async-start | bytes 4456448 | tf_op jit(solution)/shard_map/all_gather | solution.py:15
  79.8 1.2 copy-start
Sparse Core Ops, SparseCore 0:
  9.5 49.0 all-gather.5
  82.1 43.7 all-gather.3
where the time goes:
time: 141 us
  waiting for transfers between devices  92.6 us (66%)
  matrix products  17.5 us (12%)
  local copies, waits for them, and re-layouts  14.4 us (10%)
  between operations  14.3 us (10%)
  other arithmetic  1.79 us (1%)
    all_gather x1, waiting for transfers between devices, shards(): lax.all_gather(hamiltonian[:, 0], 'narrow', axis=0, tiled=True)  48.9 us
    all_gather x1, waiting for transfers between devices, in_one_piece(): out = lax.all_gather(both, axis, axis=dim, tiled=True)  43.7 us
    dot_general x8, matrix products, product(): return jnp.matmul(left, right, precision=lax.Precision.HIGHEST)  17.5 us
    split x1, local copies, waits for them, and re-layouts, in_one_piece(): jnp.split(out, [sum(widths[:k]) for k in range(1, len(widths))], axis=along)  3.92 us
  transfers between devices with their start and end apart: 2, of which 2 were waited for; matrix products, arithmetic and copies ran while one was open for 1% of the time, Pallas kernels for 0%

commit v1 on v0

v1 whole, which is shorter than its diff:
```python
import functools

import jax
import jax.numpy as jnp
from jax import lax
from jax.experimental import pallas as pl
from jax.experimental.pallas import tpu as pltpu
from jax.sharding import PartitionSpec as P

ITERS = 4
EPSILON = 1e-06
BLK = 128
ORDER = 3 * BLK
PEERS = 16
STRIP = BLK // PEERS
F32 = jnp.float32
BF16 = jnp.bfloat16
ALL, FIRST, REST = slice(0, ORDER), slice(0, BLK), slice(BLK, ORDER)


def halves(x):
    high = x.astype(BF16)
    return high, (x - high.astype(F32)).astype(BF16)


def product(left, right):
    lh, ll = left
    rh, rl = right
    return jnp.dot(
        jnp.concatenate([lh, ll, lh], axis=1),
        jnp.concatenate([rh, rh, rl], axis=0),
        preferred_element_type=F32,
    )


def kernel(
    ham, old, nbr, live, pot, out,
    packed, note, got_strip, got_note, pick, whole,
    x_all, xh_all, xl_all, sh_all, sl_all,
    edge, got_edge, pick_edge, whole_edge, rows_out,
    send, recv,
):
    w = lax.axis_index("wide")
    n = lax.axis_index("narrow")

    def peer(j):
        return (w, (n + j) & (PEERS - 1))

    barrier = pltpu.get_barrier_semaphore()

    def greet(j, _):
        pl.semaphore_signal(barrier, inc=1, device_id=peer(j), device_id_type=pl.DeviceIdType.MESH)
        return _

    lax.fori_loop(1, PEERS, greet, 0)

    forward = nbr[0, 2] == 2 * n + 1
    a = jnp.where(forward, 0, 1)
    b = 1 - a
    prev_off = ((nbr[a, 1] >> 1) - n) & (PEERS - 1)
    next_off = ((nbr[b, 2] >> 1) - n) & (PEERS - 1)

    row = lax.broadcasted_iota(jnp.int32, (BLK, BLK), 0)
    col = lax.broadcasted_iota(jnp.int32, (BLK, BLK), 1)
    diagonal = row == col
    on_a = ham[a, 0]
    on_b = ham[b, 0]
    packed[...] = jnp.where(col >= row, on_a, on_b).reshape(PEERS, STRIP, BLK)
    note[0, :, 0:BLK] = jnp.sum(jnp.where(diagonal, on_b, 0.0), axis=0, keepdims=True)
    note[0, :, BLK : 2 * BLK] = jnp.full((1, BLK), prev_off, jnp.int32).astype(F32)
    note[0, :, 2 * BLK : 3 * BLK] = jnp.full((1, BLK), next_off, jnp.int32).astype(F32)

    def push(src, dst, which, j):
        return pltpu.make_async_remote_copy(
            src_ref=src, dst_ref=dst, send_sem=send.at[which], recv_sem=recv.at[which],
            device_id=peer(j), device_id_type=pl.DeviceIdType.MESH,
        )

    def wait_all(ref, sem):
        many = ref.at[pl.ds(1, PEERS - 1)]
        pltpu.make_async_copy(many, many, sem).wait()

    pl.semaphore_wait(barrier, PEERS - 1)

    def first(j, _):
        push(note.at[0], got_note.at[j], 1, j).start()
        push(packed.at[(n + j) & (PEERS - 1)], got_strip.at[j], 0, j).start()
        return _

    lax.fori_loop(1, PEERS, first, 0)
    got_strip[0] = packed[n]
    got_note[0] = note[0]
    wait_all(got_note, recv.at[1])
    wait_all(got_strip, recv.at[0])

    below = (
        lax.broadcasted_iota(jnp.int32, (STRIP, BLK), 1)
        < lax.broadcasted_iota(jnp.int32, (STRIP, BLK), 0) + STRIP * n
    )

    def offsets(j):
        slot = (PEERS - j) & (PEERS - 1)
        return got_note[slot, :, BLK : 2 * BLK], got_note[slot, :, 2 * BLK : 3 * BLK]

    def route(j):
        to_prev, to_next = offsets(j)
        wanted = jnp.where(below, to_prev, to_next)
        chosen = jnp.zeros((STRIP, BLK), F32)
        for k in range(PEERS):
            offset = ((-j - k) & (PEERS - 1))
            chosen = jnp.where(wanted == offset, got_strip[k], chosen)
        return chosen

    for j in range(1, PEERS):
        pick[j] = route(j)
        push(pick.at[j], whole.at[n], 2, j).start()
    whole[n] = route(0)

    to_prev, to_next = offsets(0)
    far_diag = jnp.zeros((1, BLK), F32)
    for k in range(PEERS):
        far_diag = jnp.where(to_prev == ((-k) & (PEERS - 1)), got_note[k, :, 0:BLK], far_diag)

    wait_all(whole, recv.at[2])
    upper = whole[...].reshape(BLK, BLK)
    mirror = upper.T
    on_next = jnp.where(col >= row, upper, mirror)
    on_prev = jnp.where(col < row, upper, mirror)
    on_prev = jnp.where(diagonal, far_diag, on_prev)

    level = jnp.where(diagonal, pot[0], 0.0)

    def block(s):
        return x_all.at[s], xh_all.at[s], xl_all.at[s], sh_all.at[s], sl_all.at[s]

    def put(high, low, rows, cols, value):
        high[rows, cols], low[rows, cols] = halves(value)

    def assemble(s, here, before, behind):
        x, xh, xl, sh, sl = block(s)
        index = a if s == 0 else b
        t1, t2 = ham[index, 1], ham[index, 2]
        t1t = t1.T
        t2t = t2.T
        d0, d1, d2 = here - level, before - level, behind - level

        def sums(*tiles):
            return functools.reduce(jnp.add, [jnp.sum(jnp.abs(t), axis=0, keepdims=True) for t in tiles])

        most = jnp.maximum(jnp.maximum(sums(d0, t1t, t2t), sums(t1, d1)), sums(t2, d2))
        scale = 1.0 / (jnp.max(most, axis=1, keepdims=True) + EPSILON)
        tiles = ((d0, t1, t2), (t1t, d1, None), (t2t, None, d2))
        for i in range(3):
            for k in range(3):
                rows, cols = slice(BLK * i, BLK * i + BLK), slice(BLK * k, BLK * k + BLK)
                if tiles[i][k] is None:
                    value = jnp.zeros((BLK, BLK), F32)
                else:
                    value = tiles[i][k] * scale
                x[rows, cols] = value
                put(xh, xl, rows, cols, value)

    def mirrored(high, low, rest):
        put(high, low, slice(BLK, 2 * BLK), FIRST, rest[0:BLK, 0:BLK].T)
        put(high, low, slice(2 * BLK, 3 * BLK), FIRST, rest[0:BLK, BLK : 2 * BLK].T)

    def square(s):
        x, xh, xl, sh, sl = block(s)
        rest = product((xh[...], xl[...]), (xh[:, REST], xl[:, REST]))
        put(sh, sl, ALL, REST, rest)
        corner = product((xh[FIRST, :], xl[FIRST, :]), (xh[:, FIRST], xl[:, FIRST]))
        put(sh, sl, FIRST, FIRST, corner)
        mirrored(sh, sl, rest)

    def advance(s):
        x, xh, xl, sh, sl = block(s)
        rest = 1.5 * x[:, REST] - 0.5 * product((xh[...], xl[...]), (sh[:, REST], sl[:, REST]))
        x[:, REST] = rest
        corner = 1.5 * x[FIRST, FIRST] - 0.5 * product(
            (xh[FIRST, :], xl[FIRST, :]), (sh[:, FIRST], sl[:, FIRST])
        )
        x[FIRST, FIRST] = corner
        put(xh, xl, ALL, REST, rest)
        put(xh, xl, FIRST, FIRST, corner)
        mirrored(xh, xl, rest)

    def finish(s):
        x, xh, xl, sh, sl = block(s)
        whole_x = (xh[...], xl[...])
        thin = product((xh[FIRST, :], xl[FIRST, :]), whole_x)
        rows_out[s] = 1.5 * x[FIRST, :] - 0.5 * product(halves(thin), whole_x)

    assemble(0, on_a, on_prev, on_b)
    assemble(1, on_b, on_a, on_next)
    for sweep in range(ITERS - 1):
        square(0)
        square(1)
        advance(0)
        advance(1)
    finish(0)
    finish(1)

    unit = jnp.where(diagonal, 1.0, 0.0)

    def fresh(s, j):
        index = a if s == 0 else b
        x = rows_out[s, :, BLK * j : BLK * j + BLK]
        new = 0.5 * (unit - x) if j == 0 else -0.5 * x
        return jnp.where(live[index] == 1, new, old[index, j].T)

    f1a, f2b = fresh(0, 1), fresh(1, 2)
    edge[:, 0:STRIP, :] = f1a.reshape(PEERS, STRIP, BLK)
    edge[:, STRIP : 2 * STRIP, :] = f2b.reshape(PEERS, STRIP, BLK)

    def second(j, _):
        push(edge.at[(n + j) & (PEERS - 1)], got_edge.at[j], 3, j).start()
        return _

    lax.fori_loop(1, PEERS, second, 0)
    got_edge[0] = edge[n]
    wait_all(got_edge, recv.at[3])

    def route_edge(j):
        to_prev, to_next = offsets(j)
        to_prev = jnp.broadcast_to(to_prev, (STRIP, BLK))
        to_next = jnp.broadcast_to(to_next, (STRIP, BLK))
        from_prev = jnp.zeros((STRIP, BLK), F32)
        from_next = jnp.zeros((STRIP, BLK), F32)
        for k in range(PEERS):
            offset = ((-j - k) & (PEERS - 1))
            from_prev = jnp.where(to_prev == offset, got_edge[k, STRIP : 2 * STRIP], from_prev)
            from_next = jnp.where(to_next == offset, got_edge[k, 0:STRIP], from_next)
        return from_prev, from_next

    for j in range(1, PEERS):
        pick_edge[j, 0:STRIP], pick_edge[j, STRIP : 2 * STRIP] = route_edge(j)
        push(pick_edge.at[j], whole_edge.at[n], 4, j).start()
    whole_edge[n, 0:STRIP], whole_edge[n, STRIP : 2 * STRIP] = route_edge(0)

    f0a, f2a, f0b, f1b = fresh(0, 0), fresh(0, 2), fresh(1, 0), fresh(1, 1)

    def emit(j, of_a, of_b):
        out[0, j] = jnp.where(forward, of_a, of_b)
        out[1, j] = jnp.where(forward, of_b, of_a)

    emit(0, 0.5 * (f0a + f0a.T), 0.5 * (f0b + f0b.T))
    inner = 0.5 * (f2a.T + f1b)
    f1at, f2bt, innert = f1a.T, f2b.T, inner.T

    wait_all(whole_edge, recv.at[4])
    outer_a = 0.5 * (f1at + whole_edge[:, 0:STRIP, :].reshape(BLK, BLK))
    outer_b = 0.5 * (f2bt + whole_edge[:, STRIP : 2 * STRIP, :].reshape(BLK, BLK))
    emit(1, outer_a, innert)
    emit(2, inner, outer_b)

    wait_all(got_strip, send.at[0])
    wait_all(got_note, send.at[1])
    wait_all(pick, send.at[2])
    wait_all(got_edge, send.at[3])
    wait_all(pick_edge, send.at[4])


def shards(hamiltonian, old_density, neighbours, live, potential):
    vmem = pl.BlockSpec(memory_space=pltpu.VMEM)
    smem = pl.BlockSpec(memory_space=pltpu.SMEM)
    return pl.pallas_call(
        kernel,
        out_shape=jax.ShapeDtypeStruct((2, 3, BLK, BLK), F32),
        in_specs=[vmem, vmem, smem, smem, smem],
        out_specs=vmem,
        scratch_shapes=[
            pltpu.VMEM((PEERS, STRIP, BLK), F32),
            pltpu.VMEM((1, 1, 3 * BLK), F32),
            pltpu.VMEM((PEERS, STRIP, BLK), F32),
            pltpu.VMEM((PEERS, 1, 3 * BLK), F32),
            pltpu.VMEM((PEERS, STRIP, BLK), F32),
            pltpu.VMEM((PEERS, STRIP, BLK), F32),
            pltpu.VMEM((2, ORDER, ORDER), F32),
            pltpu.VMEM((2, ORDER, ORDER), BF16),
            pltpu.VMEM((2, ORDER, ORDER), BF16),
            pltpu.VMEM((2, ORDER, ORDER), BF16),
            pltpu.VMEM((2, ORDER, ORDER), BF16),
            pltpu.VMEM((PEERS, 2 * STRIP, BLK), F32),
            pltpu.VMEM((PEERS, 2 * STRIP, BLK), F32),
            pltpu.VMEM((PEERS, 2 * STRIP, BLK), F32),
            pltpu.VMEM((PEERS, 2 * STRIP, BLK), F32),
            pltpu.VMEM((2, BLK, ORDER), F32),
            pltpu.SemaphoreType.DMA((5,)),
            pltpu.SemaphoreType.DMA((5,)),
        ],
        compiler_params=pltpu.CompilerParams(
            collective_id=0, has_side_effects=True, vmem_limit_bytes=48 * 2**20
        ),
        name="density",
    )(hamiltonian, old_density, neighbours, live, potential)


def solution(mesh):
    placed = (
        P(("wide", "narrow"), None, None, None),
        P(("wide", "narrow"), None, None, None),
        P(("wide", "narrow"), None),
        P(("wide", "narrow")),
        P(),
    )
    return jax.shard_map(
        shards,
        mesh=mesh,
        in_specs=placed,
        out_specs=P(("wide", "narrow"), None, None, None),
        check_vma=False,
    )
```

time: 141 us -> 44.6 us (0.32)
  waiting for transfers between devices: 92.6 us -> 0 us
  Pallas kernels: 0 us -> 41 us
  matrix products: 17.5 us -> 0 us
  between operations: 14.3 us -> 0.71 us
  local copies, waits for them, and re-layouts: 14.4 us -> 2.74 us
  other arithmetic: 1.79 us -> 0 us
    all_gather x2 -> x0, waiting for transfers between devices: 92.6 us -> none  [the longest x1 48.9 us: shards(): lax.all_gather(hamiltonian[:, 0], 'narrow', axis=0, tiled=True)]
    pallas_call x0 -> x1, Pallas kernels: none -> 41 us  [shards(): pl.pallas_call(kernel, out_shape=jax.ShapeDtypeStruct((2, 3, BLK, BLK), F...]
    dot_general x8 -> x0, matrix products: 17.5 us -> none  [product(): return jnp.matmul(left, right, precision=lax.Precision.HIGHEST)]
    gather x5 -> x0, local copies, waits for them, and re-layouts: 7.08 us -> none  [the longest x1 2.15 us: shards(): prev_onsite = jnp.take(cluster_onsite, neighbours[:, 1], axis=0)]
    split x1 -> x0, local copies, waits for them, and re-layouts: 3.92 us -> none  [in_one_piece(): jnp.split(out, [sum(widths[:k]) for k in range(1, len(widths))], axis=along)]
    unnamed x8 -> x9, local copies, waits for them, and re-layouts: 0.2 us -> 2.74 us
    squeeze x4 -> x0, local copies, waits for them, and re-layouts: 1.98 us -> none  [the longest x1 1.77 us: assemble(): row_tiles[..., 0, :, :]]
  transfers between devices with their start and end apart: 2 -> 0, of which waited for: 2 -> 0; matrix products, arithmetic and copies ran while one was open for 1% -> 0% of each run, Pallas kernels for 0% -> 0%
where the time goes in v1:
time: 44.6 us; the launch traced here: 44.4 us
  Pallas kernels  41 us (92%)
  local copies, waits for them, and re-layouts  2.74 us (6%)
  between operations  0.71 us (2%)
    pallas_call x1, Pallas kernels, shards(): pl.pallas_call(kernel, out_shape=jax.ShapeDtypeStruct((2, 3, BLK, BLK), F...  41 us
    unnamed x9, local copies, waits for them, and re-layouts  2.74 us

profile of v1, /device:TPU:1, one launch (start us, length us, event | category | flops | bytes accessed | tf_op | source)
XLA Modules:
  0.0 44.4 jit_solution(3875188353311955819)
XLA Ops:
  0.0 0.0 copy-start.3
  0.0 0.0 copy-start.2
  0.7 0.0 copy-done.3
  0.7 0.0 copy-done.2
  0.7 0.0 copy-start
  0.7 1.0 %copy-done = f32[2,3,128,128]{3,2,1,0:T(8,128)S(1)} copy-done((f32[2,3,128,128]{3,2,1,0:T(8,128)S(1)}, f32[2,3,128,128]{3,2,1,0:T(8,128)}, u32[]{:S(2)}) %copy-start) | copy-done | bytes 393240
  1.7 0.0 copy-start.1
  1.7 1.0 %copy-done.1 = f32[2,3,128,128]{3,2,1,0:T(8,128)S(1)} copy-done((f32[2,3,128,128]{3,2,1,0:T(8,128)S(1)}, f32[2,3,128,128]{3,2,1,0:T(8,128)}, u32[]{:S(2)}) %copy-start.1) | copy-done | bytes 393240
  2.7 41.0 %density.1 = f32[2,3,128,128]{3,2,1,0:T(8,128)S(1)} custom-call(f32[2,3,128,128]{3,2,1,0:T(8,128)S(1)} %copy-done, f32[2,3,128,128]{3,2,1,0:T(8,128)S(1)} %copy-done.1, s32[2,3]{1,0:T(2,128)S(1)} %copy-done.2, s32[2]{0:T(128)S(1)} %copy-done.3, f32[1]{0:T(128)S(6)} %copy.7.pot), custom_call_target="tpu_custom_call" | custom-call | tf_op jit(solution)/shard_map/density/pallas_call | solution.py:266
  43.7 0.7 %copy.8 = f32[2,3,128,128]{3,2,1,0:T(8,128)} copy(f32[2,3,128,128]{3,2,1,0:T(8,128)S(1)} %density.1) | data formatting | bytes 786432
Async XLA Ops:
  0.0 0.7 %copy-start.3 = (s32[2]{0:T(128)S(1)}, s32[2]{0:T(128)}, u32[]{:S(2)}) copy-start(s32[2]{0:T(128)} %live.1) | copy-start | bytes 28
  0.0 0.7 %copy-start.2 = (s32[2,3]{1,0:T(2,128)S(1)}, s32[2,3]{1,0:T(2,128)}, u32[]{:S(2)}) copy-start(s32[2,3]{1,0:T(2,128)} %nbr.1) | copy-start | bytes 76
  0.7 1.0 %copy-start = (f32[2,3,128,128]{3,2,1,0:T(8,128)S(1)}, f32[2,3,128,128]{3,2,1,0:T(8,128)}, u32[]{:S(2)}) copy-start(f32[2,3,128,128]{3,2,1,0:T(8,128)} %ham.1) | copy-start | bytes 1179652
  1.7 1.0 %copy-start.1 = (f32[2,3,128,128]{3,2,1,0:T(8,128)S(1)}, f32[2,3,128,128]{3,2,1,0:T(8,128)}, u32[]{:S(2)}) copy-start(f32[2,3,128,128]{3,2,1,0:T(8,128)} %old.1) | copy-start | bytes 1179652

commit v2 on v1

v2 whole, which is shorter than its diff:
```python
import functools

import jax
import jax.numpy as jnp
from jax import lax
from jax.experimental import pallas as pl
from jax.experimental.pallas import tpu as pltpu
from jax.sharding import PartitionSpec as P

ITERS = 4
EPSILON = 1e-06
BLK = 128
ORDER = 3 * BLK
PEERS = 16
STRIP = BLK // PEERS
F32 = jnp.float32
BF16 = jnp.bfloat16
ALL, FIRST = slice(0, ORDER), slice(0, BLK)


def halves(x):
    high = x.astype(BF16)
    return high, (x - high.astype(F32)).astype(BF16)


def product(left, right):
    lh, ll = left
    rh, rl = right
    return jnp.dot(
        jnp.concatenate([lh, ll, lh], axis=1),
        jnp.concatenate([rh, rh, rl], axis=0),
        preferred_element_type=F32,
    )


def kernel(
    ham_hbm, old_hbm, nbr_hbm, live_hbm, pot_hbm, out,
    ham, old, nbr, live, pot,
    packed, outer, note, got_packed, got_outer, got_note,
    pick_near, pick_far, near, far, turned,
    x_all, xh_all, xl_all, sh_all, sl_all,
    load, send, recv,
):
    w = lax.axis_index("wide")
    n = lax.axis_index("narrow")

    def peer(j):
        return (w, (n + j) & (PEERS - 1))

    inputs = ((nbr_hbm, nbr), (ham_hbm, ham), (live_hbm, live), (old_hbm, old), (pot_hbm, pot))
    loads = [pltpu.make_async_copy(src, dst, load.at[i]) for i, (src, dst) in enumerate(inputs)]
    for copy in loads:
        copy.start()

    barrier = pltpu.get_barrier_semaphore()

    def greet(j, _):
        pl.semaphore_signal(barrier, inc=1, device_id=peer(j), device_id_type=pl.DeviceIdType.MESH)
        return _

    lax.fori_loop(1, PEERS, greet, 0)

    for copy in loads:
        copy.wait()

    forward = nbr[0, 2] == 2 * n + 1
    a = jnp.where(forward, 0, 1)
    b = 1 - a
    live_a, live_b = live[a], live[b]

    row = lax.broadcasted_iota(jnp.int32, (BLK, BLK), 0)
    col = lax.broadcasted_iota(jnp.int32, (BLK, BLK), 1)
    diagonal = row == col
    on_a = ham[a, 0]
    on_b = ham[b, 0]
    packed[...] = jnp.where(col >= row, on_a, on_b).reshape(PEERS, STRIP, BLK)
    outer[:, 0:STRIP] = jnp.where(live_a == 1, ham[a, 2], old[a, 1]).reshape(PEERS, STRIP, BLK)
    outer[:, STRIP : 2 * STRIP] = jnp.where(live_b == 1, ham[b, 1], old[b, 2]).reshape(PEERS, STRIP, BLK)
    note[0, :, 0:BLK] = jnp.sum(jnp.where(diagonal, on_b, 0.0), axis=0, keepdims=True)
    facts = (
        ((nbr[a, 1] >> 1) - n) & (PEERS - 1), ((nbr[b, 2] >> 1) - n) & (PEERS - 1), live_a, live_b,
    )
    for i, fact in enumerate(facts):
        note[0, :, BLK * (i + 1) : BLK * (i + 2)] = jnp.full((1, BLK), fact, jnp.int32).astype(F32)

    def push(src, dst, which, j):
        return pltpu.make_async_remote_copy(
            src_ref=src, dst_ref=dst, send_sem=send.at[which], recv_sem=recv.at[which],
            device_id=peer(j), device_id_type=pl.DeviceIdType.MESH,
        )

    def wait_all(ref, sem):
        many = ref.at[pl.ds(1, PEERS - 1)]
        pltpu.make_async_copy(many, many, sem).wait()

    pl.semaphore_wait(barrier, PEERS - 1)

    def first(j, _):
        push(note.at[0], got_note.at[j], 0, j).start()
        push(packed.at[(n + j) & (PEERS - 1)], got_packed.at[j], 1, j).start()
        return _

    lax.fori_loop(1, PEERS, first, 0)

    def second(j, _):
        push(outer.at[(n + j) & (PEERS - 1)], got_outer.at[j], 2, j).start()
        return _

    lax.fori_loop(1, PEERS, second, 0)
    got_packed[0] = packed[n]
    got_note[0] = note[0]
    got_outer[0] = outer[n]

    level = jnp.where(diagonal, pot[0], 0.0)
    turned[0] = ham[a, 1].T
    turned[1] = ham[b, 2].T

    wait_all(got_note, recv.at[0])
    wait_all(got_packed, recv.at[1])

    below = (
        lax.broadcasted_iota(jnp.int32, (STRIP, BLK), 1)
        < lax.broadcasted_iota(jnp.int32, (STRIP, BLK), 0) + STRIP * n
    )

    def part(slot, i):
        return got_note[slot, :, BLK * i : BLK * (i + 1)]

    def offsets(j):
        slot = (PEERS - j) & (PEERS - 1)
        return (
            jnp.broadcast_to(part(slot, 1), (STRIP, BLK)),
            jnp.broadcast_to(part(slot, 2), (STRIP, BLK)),
        )

    def select(j, wanted, slots):
        chosen = slots(0)
        for k in range(1, PEERS):
            chosen = jnp.where(wanted == ((-j - k) & (PEERS - 1)), slots(k), chosen)
        return chosen

    def route_near(j):
        to_prev, to_next = offsets(j)
        return select(j, jnp.where(below, to_prev, to_next), lambda k: got_packed[k])

    for j in range(1, PEERS):
        pick_near[j] = route_near(j)
        push(pick_near.at[j], near.at[n], 3, j).start()
    near[n] = route_near(0)

    wait_all(got_outer, recv.at[2])

    def route_far(j, ref):
        to_prev, to_next = offsets(j)
        ref[0:STRIP] = select(j, jnp.where(below, to_next, to_prev), lambda k: got_packed[k])
        ref[STRIP : 2 * STRIP] = select(j, to_prev, lambda k: got_outer[k, STRIP : 2 * STRIP])
        ref[2 * STRIP : 3 * STRIP] = select(j, to_next, lambda k: got_outer[k, 0:STRIP])

    for j in range(1, PEERS):
        route_far(j, pick_far.at[j])
        push(pick_far.at[j], far.at[n], 4, j).start()
    route_far(0, far.at[n])

    def noted(i, which):
        return select(0, part(0, which), lambda k: part(k, i))

    diag_prev, diag_next = noted(0, 1), noted(0, 2)
    live_prev, live_next = noted(4, 1), noted(3, 2)

    def unpack(tile, low_diag):
        mirror = tile.T
        high = jnp.where(col >= row, tile, mirror)
        low = jnp.where(diagonal, low_diag, jnp.where(col < row, tile, mirror))
        return high, low

    wait_all(near, recv.at[3])
    on_next, on_prev = unpack(near[...].reshape(BLK, BLK), diag_prev)

    def block(s):
        return x_all.at[s], xh_all.at[s], xl_all.at[s], sh_all.at[s], sl_all.at[s]

    def tile(i):
        return slice(BLK * i, BLK * i + BLK)

    def put(high, low, rows, cols, value):
        high[rows, cols], low[rows, cols] = halves(value)

    def assemble(s, here, before, behind, t1, t1t, t2, t2t):
        x, xh, xl, sh, sl = block(s)
        d0, d1, d2 = here - level, before - level, behind - level

        def sums(*tiles):
            return functools.reduce(jnp.add, [jnp.sum(jnp.abs(t), axis=0, keepdims=True) for t in tiles])

        most = jnp.maximum(jnp.maximum(sums(d0, t1t, t2t), sums(t1, d1)), sums(t2, d2))
        scale = 1.0 / (jnp.max(most, axis=1, keepdims=True) + EPSILON)
        tiles = ((d0, t1, t2), (t1t, d1, None), (t2t, None, d2))
        for i in range(3):
            for k in range(3):
                rows, cols = tile(i), tile(k)
                if tiles[i][k] is None:
                    value = jnp.zeros((BLK, BLK), F32)
                else:
                    value = tiles[i][k] * scale
                x[rows, cols] = value
                put(xh, xl, rows, cols, value)

    def symmetric(left, right):
        lh, ll = left
        rh, rl = right

        def pair(ref, i):
            return jnp.concatenate([ref[:, tile(i)], ref[:, tile((i + 1) % 3)]], axis=1)

        return [
            product((lh[tile(i), :], ll[tile(i), :]), (pair(rh, i), pair(rl, i))) for i in range(3)
        ]

    def square(s):
        x, xh, xl, sh, sl = block(s)
        for i, both in enumerate(symmetric((xh, xl), (xh, xl))):
            here, after = tile(i), tile((i + 1) % 3)
            put(sh, sl, here, here, both[:, 0:BLK])
            put(sh, sl, here, after, both[:, BLK : 2 * BLK])
            put(sh, sl, after, here, both[:, BLK : 2 * BLK].T)

    def advance(s):
        x, xh, xl, sh, sl = block(s)
        for i, both in enumerate(symmetric((xh, xl), (sh, sl))):
            here, after = tile(i), tile((i + 1) % 3)
            own = 1.5 * x[here, here] - 0.5 * both[:, 0:BLK]
            side = 1.5 * x[here, after] - 0.5 * both[:, BLK : 2 * BLK]
            turn = side.T
            x[here, here] = own
            x[here, after] = side
            if i == 2:
                x[after, here] = turn
            put(xh, xl, here, here, own)
            put(xh, xl, here, after, side)
            put(xh, xl, after, here, turn)

    def finish(s, cols):
        x, xh, xl, sh, sl = block(s)
        thin = product((xh[FIRST, :], xl[FIRST, :]), (xh[...], xl[...]))
        return 1.5 * x[FIRST, cols] - 0.5 * product(halves(thin), (xh[:, cols], xl[:, cols]))

    def iterate(s, t):
        for sweep in range(ITERS - 1):
            square(s)
            square(t)
            advance(s)
            advance(t)

    assemble(0, on_a, on_prev, on_b, ham[a, 1], turned[0], ham[a, 2], ham[b, 1])
    assemble(1, on_b, on_a, on_next, ham[b, 1], ham[a, 2], ham[b, 2], turned[1])
    iterate(0, 1)
    new_a, new_b = finish(0, ALL), finish(1, ALL)

    unit = jnp.where(diagonal, 1.0, 0.0)

    def fresh(new, index, j):
        x = new[:, tile(j)]
        value = 0.5 * (unit - x) if j == 0 else -0.5 * x
        return jnp.where(live[index] == 1, value, old[index, j].T)

    f0a, f1a, f2a = [fresh(new_a, a, j) for j in range(3)]
    f0b, f1b, f2b = [fresh(new_b, b, j) for j in range(3)]

    def emit(j, of_a, of_b):
        out[0, j] = jnp.where(forward, of_a, of_b)
        out[1, j] = jnp.where(forward, of_b, of_a)

    emit(0, 0.5 * (f0a + f0a.T), 0.5 * (f0b + f0b.T))
    inner = 0.5 * (f2a.T + f1b)
    out[0, 1] = f1a.T
    out[1, 1] = inner.T
    out[0, 2] = inner
    out[1, 2] = f2b.T

    wait_all(far, recv.at[4])
    on_prev_prev, on_next_next = unpack(far[:, 0:STRIP].reshape(BLK, BLK), diag_next)
    far_prev = far[:, STRIP : 2 * STRIP].reshape(BLK, BLK)
    far_next = far[:, 2 * STRIP : 3 * STRIP].reshape(BLK, BLK)
    far_prev_t, far_next_t = far_prev.T, far_next.T
    on_next, on_prev = unpack(near[...].reshape(BLK, BLK), diag_prev)
    assemble(2, on_prev, on_prev_prev, on_a, far_prev, far_prev_t, turned[0], ham[a, 1])
    assemble(3, on_next, on_b, on_next_next, turned[1], ham[b, 2], far_next, far_next_t)
    iterate(2, 3)
    edge_prev = jnp.where(live_prev == 1.0, -0.5 * finish(2, tile(2)), far_prev_t)
    edge_next = jnp.where(live_next == 1.0, -0.5 * finish(3, tile(1)), far_next_t)
    outer_a = 0.5 * (out[0, 1] + edge_prev)
    outer_b = 0.5 * (out[1, 2] + edge_next)
    emit(1, outer_a, out[1, 1])
    emit(2, out[0, 2], outer_b)

    wait_all(got_note, send.at[0])
    wait_all(got_packed, send.at[1])
    wait_all(got_outer, send.at[2])
    wait_all(near, send.at[3])
    wait_all(far, send.at[4])


def shards(hamiltonian, old_density, neighbours, live, potential):
    hbm = pl.BlockSpec(memory_space=pltpu.HBM)
    strips = pltpu.VMEM((PEERS, STRIP, BLK), F32)
    two_strips = pltpu.VMEM((PEERS, 2 * STRIP, BLK), F32)
    three_strips = pltpu.VMEM((PEERS, 3 * STRIP, BLK), F32)
    matrices = pltpu.VMEM((4, ORDER, ORDER), F32)
    matrix_halves = pltpu.VMEM((4, ORDER, ORDER), BF16)
    return pl.pallas_call(
        kernel,
        out_shape=jax.ShapeDtypeStruct((2, 3, BLK, BLK), F32),
        in_specs=[hbm] * 5,
        out_specs=pl.BlockSpec(memory_space=pltpu.VMEM),
        scratch_shapes=[
            pltpu.VMEM((2, 3, BLK, BLK), F32),
            pltpu.VMEM((2, 3, BLK, BLK), F32),
            pltpu.SMEM((2, 3), jnp.int32),
            pltpu.SMEM((2,), jnp.int32),
            pltpu.SMEM((1,), F32),
            strips, two_strips, pltpu.VMEM((1, 1, 5 * BLK), F32),
            strips, two_strips, pltpu.VMEM((PEERS, 1, 5 * BLK), F32),
            strips, three_strips, strips, three_strips,
            pltpu.VMEM((2, BLK, BLK), F32),
            matrices, matrix_halves, matrix_halves, matrix_halves, matrix_halves,
            pltpu.SemaphoreType.DMA((5,)),
            pltpu.SemaphoreType.DMA((5,)),
            pltpu.SemaphoreType.DMA((5,)),
        ],
        compiler_params=pltpu.CompilerParams(
            collective_id=0, has_side_effects=True, vmem_limit_bytes=60 * 2**20
        ),
        name="density",
    )(hamiltonian, old_density, neighbours, live, potential)


def solution(mesh):
    placed = (
        P(("wide", "narrow"), None, None, None),
        P(("wide", "narrow"), None, None, None),
        P(("wide", "narrow"), None),
        P(("wide", "narrow")),
        P(),
    )
    return jax.shard_map(
        shards,
        mesh=mesh,
        in_specs=placed,
        out_specs=P(("wide", "narrow"), None, None, None),
        check_vma=False,
    )
```

time: 44.6 us -> 36.7 us (0.82)
  Pallas kernels: 41 us -> 34.1 us
  local copies, waits for them, and re-layouts: 2.74 us -> 1.77 us
    pallas_call x1, Pallas kernels: 41 us -> 34.1 us  [shards(): pl.pallas_call(kernel, out_shape=jax.ShapeDtypeStruct((2, 3, BLK, BLK), F...]
    unnamed x9 -> x1, local copies, waits for them, and re-layouts: 2.74 us -> 1.77 us
where the time goes in v2:
time: 36.7 us; the launch traced here: 36.5 us
  Pallas kernels  34.1 us (93%)
  local copies, waits for them, and re-layouts  1.77 us (5%)
  between operations  0.66 us (2%)
    pallas_call x1, Pallas kernels, shards(): pl.pallas_call(kernel, out_shape=jax.ShapeDtypeStruct((2, 3, BLK, BLK), F...  34.1 us
    unnamed x1, local copies, waits for them, and re-layouts  1.77 us

profile of v2, /device:TPU:1, one launch (start us, length us, event | category | flops | bytes accessed | tf_op | source)
XLA Modules:
  0.0 36.5 jit_solution(15360837241016451196)
XLA Ops:
  0.7 34.1 %density.1 = f32[2,3,128,128]{3,2,1,0:T(8,128)} custom-call(f32[2,3,128,128]{3,2,1,0:T(8,128)} %ham_hbm.1, f32[2,3,128,128]{3,2,1,0:T(8,128)} %old_hbm.1, s32[2,3]{1,0:T(2,128)} %nbr_hbm.1, s32[2]{0:T(128)} %live_hbm.1, f32[1]{0:T(128)S(6)} %copy.7.pot_hbm), custom_call_target="tpu_custom_call" | custom-call | tf_op jit(solution)/shard_map/density/pallas_call | solution.py:310
  34.7 1.8 %copy.8 = f32[2,3,128,128]{3,2,1,0:T(8,128)} copy(f32[2,3,128,128]{3,2,1,0:T(8,128)} %density.1) | data formatting | bytes 786432

commit v3 on v2

v3 whole, which is shorter than its diff:
```python
import functools

import jax
import jax.numpy as jnp
from jax import lax
from jax.experimental import pallas as pl
from jax.experimental.pallas import tpu as pltpu
from jax.sharding import PartitionSpec as P

ITERS = 4
EPSILON = 1e-06
VMEM_LIMIT = 54_580 * 1024
BLK = 128
ORDER = 3 * BLK
PEERS = 16
STRIP = BLK // PEERS
FIELD = BLK // 4
ORDER_OUT = sorted(range(1, PEERS), key=lambda j: abs(j - PEERS // 2))
F32 = jnp.float32
BF16 = jnp.bfloat16
ALL, FIRST = slice(0, ORDER), slice(0, BLK)


def halves(x):
    high = x.astype(BF16)
    return high, (x - high.astype(F32)).astype(BF16)


def product(left, right):
    lh, ll = left
    rh, rl = right
    return jnp.dot(
        jnp.concatenate([lh, ll, lh], axis=1),
        jnp.concatenate([rh, rh, rl], axis=0),
        preferred_element_type=F32,
    )


def kernel(
    ham_hbm, old_hbm, nbr_hbm, live_hbm, pot_hbm, out,
    ham, old, nbr, live, pot,
    packed, outer_next, outer_prev, note, got_packed, got_next, got_prev, got_note,
    pick_near, pick_far, pick_last, near, far, last, turned, base,
    x_all, xh_all, xl_all, sh_all, sl_all,
    load, send, recv,
):
    w = lax.axis_index("wide")
    n = lax.axis_index("narrow")

    def peer(j):
        return (w, (n + j) & (PEERS - 1))

    inputs = ((nbr_hbm, nbr), (ham_hbm, ham), (live_hbm, live), (old_hbm, old), (pot_hbm, pot))
    loads = [pltpu.make_async_copy(src, dst, load.at[i]) for i, (src, dst) in enumerate(inputs)]
    for copy in loads:
        copy.start()

    barrier = pltpu.get_barrier_semaphore()

    def greet(j, _):
        pl.semaphore_signal(barrier, inc=1, device_id=peer(j), device_id_type=pl.DeviceIdType.MESH)
        return _

    lax.fori_loop(1, PEERS, greet, 0)

    for copy in loads:
        copy.wait()

    forward = nbr[0, 2] == 2 * n + 1
    a = jnp.where(forward, 0, 1)
    b = 1 - a
    live_a, live_b = live[a], live[b]

    row = lax.broadcasted_iota(jnp.int32, (BLK, BLK), 0)
    col = lax.broadcasted_iota(jnp.int32, (BLK, BLK), 1)
    diagonal = row == col
    on_a = ham[a, 0]
    on_b = ham[b, 0]
    packed[...] = jnp.where(col >= row, on_a, on_b).reshape(PEERS, STRIP, BLK)
    outer_prev[...] = jnp.where(live_a == 1, ham[a, 2], old[a, 1]).reshape(PEERS, STRIP, BLK)
    outer_next[...] = jnp.where(live_b == 1, ham[b, 1], old[b, 2]).reshape(PEERS, STRIP, BLK)
    note[0, :, 0:BLK] = jnp.sum(jnp.where(diagonal, on_b, 0.0), axis=0, keepdims=True)
    facts = (
        ((nbr[a, 1] >> 1) - n) & (PEERS - 1), ((nbr[b, 2] >> 1) - n) & (PEERS - 1), live_a, live_b,
    )
    lane = lax.broadcasted_iota(jnp.int32, (1, BLK), 1)
    told = jnp.full((1, BLK), facts[0], jnp.int32)
    for i in range(1, 4):
        told = jnp.where(lane >= FIELD * i, facts[i], told)
    note[0, :, BLK : 2 * BLK] = told.astype(F32)

    def push(src, dst, which, j):
        return pltpu.make_async_remote_copy(
            src_ref=src, dst_ref=dst, send_sem=send.at[which], recv_sem=recv.at[which],
            device_id=peer(j), device_id_type=pl.DeviceIdType.MESH,
        )

    def wait_all(ref, sem):
        many = ref.at[pl.ds(1, PEERS - 1)]
        pltpu.make_async_copy(many, many, sem).wait()

    pl.semaphore_wait(barrier, PEERS - 1)

    def to_all(*moves):
        def step(m, _):
            j = PEERS // 2 + (1 - 2 * (m & 1)) * ((m + 1) >> 1)
            for src, dst, which in moves:
                push(src.at[0 if src is note else (n + j) & (PEERS - 1)], dst.at[j], which, j).start()
            return _

        lax.fori_loop(0, PEERS - 1, step, 0)

    to_all((note, got_note, 0), (packed, got_packed, 1))
    to_all((outer_next, got_next, 2))
    to_all((outer_prev, got_prev, 3))
    got_note[0] = note[0]
    got_packed[0] = packed[n]
    got_next[0] = outer_next[n]
    got_prev[0] = outer_prev[n]

    level = jnp.where(diagonal, pot[0], 0.0)

    def block(s):
        return x_all.at[s], xh_all.at[s], xl_all.at[s], sh_all.at[s], sl_all.at[s]

    def tile(i):
        return slice(BLK * i, BLK * i + BLK)

    def put(high, low, rows, cols, value):
        high[rows, cols], low[rows, cols] = halves(value)

    def sums(*tiles):
        return functools.reduce(jnp.add, [jnp.sum(jnp.abs(t), axis=0, keepdims=True) for t in tiles])

    def scale_of(most):
        return 1.0 / (jnp.max(most, axis=1, keepdims=True) + EPSILON)

    def assemble(s, tiles):
        x, xh, xl, sh, sl = block(s)
        for i in range(3):
            for k in range(3):
                rows, cols = tile(i), tile(k)
                value = jnp.zeros((BLK, BLK), F32) if tiles[i][k] is None else tiles[i][k]
                x[rows, cols] = value
                put(xh, xl, rows, cols, value)

    def symmetric(left, right, first):
        def strip(ref, i, inner):
            return jnp.concatenate([ref[tile(i), tile(k)] for k in inner], axis=1)

        def pair(ref, i, inner):
            return jnp.concatenate([
                jnp.concatenate([ref[tile(k), tile(i)], ref[tile(k), tile((i + 1) % 3)]], axis=1)
                for k in inner
            ], axis=0)

        results = []
        for i in range(3):
            inner = (0, i) if first and i > 0 else (0, 1, 2)
            results.append(product(
                tuple(strip(ref, i, inner) for ref in left), tuple(pair(ref, i, inner) for ref in right)
            ))
        return results

    def square(s, first=False, keep=None):
        x, xh, xl, sh, sl = block(s)
        for i, both in enumerate(symmetric((xh, xl), (xh, xl), first)):
            here, after = tile(i), tile((i + 1) % 3)
            own, side = both[:, 0:BLK], both[:, BLK : 2 * BLK]
            put(sh, sl, here, here, own)
            put(sh, sl, here, after, side)
            put(sh, sl, after, here, side.T)
            if keep is not None and i == keep:
                base[s, 0] = own
            if keep is not None and i == 0 and keep == 1:
                base[s, 1] = side.T
            if keep is not None and i == 2 and keep == 2:
                base[s, 1] = side

    def complete(s, u, value):
        x, xh, xl, sh, sl = block(s)
        mine = tile(u)
        x[mine, mine] = value
        vh, vl = halves(value)
        xh[mine, mine], xl[mine, mine] = vh, vl
        more = product(
            (vh, vl),
            (
                jnp.concatenate([xh[mine, FIRST], vh], axis=1),
                jnp.concatenate([xl[mine, FIRST], vl], axis=1),
            ),
        )
        side = base[s, 1] + more[:, 0:BLK]
        put(sh, sl, mine, FIRST, side)
        put(sh, sl, FIRST, mine, side.T)
        put(sh, sl, mine, mine, base[s, 0] + more[:, BLK : 2 * BLK])

    def advance(s, scale=None):
        x, xh, xl, sh, sl = block(s)
        once, thrice = (1.5, 0.5) if scale is None else (1.5 * scale, 0.5 * scale * scale * scale)
        for i, both in enumerate(symmetric((xh, xl), (sh, sl), scale is not None)):
            here, after = tile(i), tile((i + 1) % 3)
            own = once * x[here, here] - thrice * both[:, 0:BLK]
            side = once * x[here, after] - thrice * both[:, BLK : 2 * BLK]
            turn = side.T
            x[here, here] = own
            x[here, after] = side
            if i == 2:
                x[after, here] = turn
            put(xh, xl, here, here, own)
            put(xh, xl, here, after, side)
            put(xh, xl, after, here, turn)

    def finish(s, cols):
        x, xh, xl, sh, sl = block(s)
        thin = product((xh[FIRST, :], xl[FIRST, :]), (xh[...], xl[...]))
        return 1.5 * x[FIRST, cols] - 0.5 * product(halves(thin), (xh[:, cols], xl[:, cols]))

    t1a_t, t2b_t = ham[a, 1].T, ham[b, 2].T
    turned[0] = t1a_t
    turned[1] = t2b_t
    d_a, d_b = on_a - level, on_b - level
    assemble(0, ((d_a, ham[a, 1], ham[a, 2]), (t1a_t, None, None), (ham[b, 1], None, d_b)))
    assemble(1, ((d_b, ham[b, 1], ham[b, 2]), (ham[a, 2], d_a, None), (t2b_t, None, None)))
    square(0, True, 1)
    square(1, True, 2)
    most_a = jnp.maximum(sums(d_a, t1a_t, ham[b, 1]), sums(ham[a, 2], d_b))
    most_b = jnp.maximum(sums(d_b, ham[a, 2], t2b_t), sums(ham[b, 1], d_a))
    part_a, part_b = sums(ham[a, 1]), sums(ham[b, 2])

    wait_all(got_note, recv.at[0])
    wait_all(got_packed, recv.at[1])

    below = (
        lax.broadcasted_iota(jnp.int32, (STRIP, BLK), 1)
        < lax.broadcasted_iota(jnp.int32, (STRIP, BLK), 0) + STRIP * n
    )

    def field(slot, i, rows):
        told = got_note[slot, :, BLK : 2 * BLK]
        return jnp.broadcast_to(told[:, FIELD * i : FIELD * i + 1], (rows, BLK))

    def offsets(j):
        slot = (PEERS - j) & (PEERS - 1)
        return field(slot, 0, STRIP), field(slot, 1, STRIP)

    def select(j, wanted, slots):
        chosen = slots(0)
        for k in range(1, PEERS):
            chosen = jnp.where(wanted == ((-j - k) & (PEERS - 1)), slots(k), chosen)
        return chosen

    def route_near(j):
        to_prev, to_next = offsets(j)
        return select(j, jnp.where(below, to_prev, to_next), lambda k: got_packed[k])

    for j in ORDER_OUT:
        pick_near[j] = route_near(j)
        push(pick_near.at[j], near.at[n], 4, j).start()
    near[n] = route_near(0)

    wait_all(got_next, recv.at[2])

    def route_far(j, ref):
        to_prev, to_next = offsets(j)
        ref[0:STRIP] = select(j, jnp.where(below, to_next, to_prev), lambda k: got_packed[k])
        ref[STRIP : 2 * STRIP] = select(j, to_prev, lambda k: got_next[k])

    for j in ORDER_OUT:
        route_far(j, pick_far.at[j])
        push(pick_far.at[j], far.at[n], 5, j).start()
    route_far(0, far.at[n])

    wait_all(got_prev, recv.at[3])

    def route_last(j):
        return select(j, offsets(j)[1], lambda k: got_prev[k])

    for j in ORDER_OUT:
        pick_last[j] = route_last(j)
        push(pick_last.at[j], last.at[n], 6, j).start()
    last[n] = route_last(0)

    to_prev, to_next = field(0, 0, 1), field(0, 1, 1)
    diag_prev, diag_next = [select(0, to, lambda k: got_note[k, :, 0:BLK]) for to in (to_prev, to_next)]
    live_prev = select(0, to_prev, lambda k: field(k, 3, 1))
    live_next = select(0, to_next, lambda k: field(k, 2, 1))

    def unpack(tile, low_diag):
        mirror = tile.T
        high = jnp.where(col >= row, tile, mirror)
        low = jnp.where(diagonal, low_diag, jnp.where(col < row, tile, mirror))
        return high, low

    wait_all(near, recv.at[4])
    on_next, on_prev = unpack(near[...].reshape(BLK, BLK), diag_prev)
    d_prev, d_next = on_prev - level, on_next - level
    complete(0, 1, d_prev)
    complete(1, 2, d_next)
    advance(0, scale_of(jnp.maximum(most_a, part_a + sums(d_prev))))
    advance(1, scale_of(jnp.maximum(most_b, part_b + sums(d_next))))
    for sweep in range(ITERS - 2):
        square(0)
        square(1)
        advance(0)
        advance(1)

    new_a = finish(0, ALL)
    new_b = finish(1, ALL)

    unit = jnp.where(diagonal, 1.0, 0.0)

    def fresh(new, index, j):
        x = new[:, tile(j)]
        value = 0.5 * (unit - x) if j == 0 else -0.5 * x
        return jnp.where(live[index] == 1, value, old[index, j].T)

    f0a, f1a, f2a = [fresh(new_a, a, j) for j in range(3)]
    f0b, f1b, f2b = [fresh(new_b, b, j) for j in range(3)]

    def emit(j, of_a, of_b):
        out[0, j] = jnp.where(forward, of_a, of_b)
        out[1, j] = jnp.where(forward, of_b, of_a)

    emit(0, 0.5 * (f0a + f0a.T), 0.5 * (f0b + f0b.T))
    inner = 0.5 * (f2a.T + f1b)
    out[0, 1] = f1a.T
    out[1, 1] = inner.T
    out[0, 2] = inner
    out[1, 2] = f2b.T

    wait_all(far, recv.at[5])
    wait_all(last, recv.at[6])
    on_prev_prev, on_next_next = unpack(far[:, 0:STRIP].reshape(BLK, BLK), diag_next)
    far_prev = far[:, STRIP : 2 * STRIP].reshape(BLK, BLK)
    far_prev_t = far_prev.T
    d_prev_prev = on_prev_prev - level
    on_next, on_prev = unpack(near[...].reshape(BLK, BLK), diag_prev)
    d_prev, d_next, d_a, d_b = on_prev - level, on_next - level, on_a - level, on_b - level
    assemble(2, ((d_prev, far_prev, turned[0]), (far_prev_t, d_prev_prev, None), (ham[a, 1], None, d_a)))
    scale_prev = scale_of(jnp.maximum(
        jnp.maximum(sums(d_prev, far_prev_t, ham[a, 1]), sums(far_prev, d_prev_prev)), sums(turned[0], d_a)
    ))
    far_next = last[...].reshape(BLK, BLK)
    far_next_t = far_next.T
    d_next_next = on_next_next - level
    assemble(3, ((d_next, turned[1], far_next), (ham[b, 2], d_b, None), (far_next_t, None, d_next_next)))
    scale_next = scale_of(jnp.maximum(
        jnp.maximum(sums(d_next, ham[b, 2], far_next_t), sums(turned[1], d_b)), sums(far_next, d_next_next)
    ))
    square(2, True)
    square(3, True)
    advance(2, scale_prev)
    advance(3, scale_next)
    for sweep in range(ITERS - 2):
        square(2)
        square(3)
        advance(2)
        advance(3)
    edge_prev = jnp.where(live_prev == 1.0, -0.5 * finish(2, tile(2)), far[:, STRIP : 2 * STRIP].reshape(BLK, BLK).T)
    edge_next = jnp.where(live_next == 1.0, -0.5 * finish(3, tile(1)), last[...].reshape(BLK, BLK).T)
    outer_a = 0.5 * (out[0, 1] + edge_prev)
    outer_b = 0.5 * (out[1, 2] + edge_next)
    emit(1, outer_a, out[1, 1])
    emit(2, out[0, 2], outer_b)

    for i, ref in enumerate((got_note, got_packed, got_next, got_prev, near, far, last)):
        wait_all(ref, send.at[i])


def shards(hamiltonian, old_density, neighbours, live, potential):
    hbm = pl.BlockSpec(memory_space=pltpu.HBM)
    strips = pltpu.VMEM((PEERS, STRIP, BLK), F32)
    two_strips = pltpu.VMEM((PEERS, 2 * STRIP, BLK), F32)
    matrices = pltpu.VMEM((4, ORDER, ORDER), F32)
    matrix_halves = pltpu.VMEM((4, ORDER, ORDER), BF16)
    return pl.pallas_call(
        kernel,
        out_shape=jax.ShapeDtypeStruct((2, 3, BLK, BLK), F32),
        in_specs=[hbm] * 5,
        out_specs=pl.BlockSpec(memory_space=pltpu.VMEM),
        scratch_shapes=[
            pltpu.VMEM((2, 3, BLK, BLK), F32),
            pltpu.VMEM((2, 3, BLK, BLK), F32),
            pltpu.SMEM((2, 3), jnp.int32),
            pltpu.SMEM((2,), jnp.int32),
            pltpu.SMEM((1,), F32),
            strips, strips, strips, pltpu.VMEM((1, 1, 2 * BLK), F32),
            strips, strips, strips, pltpu.VMEM((PEERS, 1, 2 * BLK), F32),
            strips, two_strips, strips, strips, two_strips, strips,
            pltpu.VMEM((2, BLK, BLK), F32),
            pltpu.VMEM((2, 2, BLK, BLK), F32),
            matrices, matrix_halves, matrix_halves, matrix_halves, matrix_halves,
            pltpu.SemaphoreType.DMA((5,)),
            pltpu.SemaphoreType.DMA((7,)),
            pltpu.SemaphoreType.DMA((7,)),
        ],
        compiler_params=pltpu.CompilerParams(
            collective_id=0, has_side_effects=True, vmem_limit_bytes=VMEM_LIMIT
        ),
        name="density",
    )(hamiltonian, old_density, neighbours, live, potential)


def solution(mesh):
    placed = (
        P(("wide", "narrow"), None, None, None),
        P(("wide", "narrow"), None, None, None),
        P(("wide", "narrow"), None),
        P(("wide", "narrow")),
        P(),
    )
    return jax.shard_map(
        shards,
        mesh=mesh,
        in_specs=placed,
        out_specs=P(("wide", "narrow"), None, None, None),
        check_vma=False,
    )
```

time: 36.7 us -> 32.6 us (0.89)
  Pallas kernels: 34.1 us -> 31 us
  local copies, waits for them, and re-layouts: 1.77 us -> 0.76 us
    pallas_call x1, Pallas kernels: 34.1 us -> 31 us  [shards(): pl.pallas_call(kernel, out_shape=jax.ShapeDtypeStruct((2, 3, BLK, BLK), F...]
    unnamed x1 -> x5, local copies, waits for them, and re-layouts: 1.77 us -> 0.76 us
where the time goes in v3:
time: 32.6 us; the launch traced here: 32.5 us
  Pallas kernels  31 us (95%)
  local copies, waits for them, and re-layouts  0.76 us (2%)
  between operations  0.7 us (2%)
    pallas_call x1, Pallas kernels, shards(): pl.pallas_call(kernel, out_shape=jax.ShapeDtypeStruct((2, 3, BLK, BLK), F...  31 us
    unnamed x5, local copies, waits for them, and re-layouts  0.76 us

profile of v3, /device:TPU:1, one launch (start us, length us, event | category | flops | bytes accessed | tf_op | source)
XLA Modules:
  0.0 32.5 jit_solution(9909322159953848628)
XLA Ops:
  0.0 0.0 copy-start.1
  0.0 0.0 copy-start
  0.7 0.0 copy-done.1
  0.7 0.0 copy-done
  0.7 31.0 %density.1 = f32[2,3,128,128]{3,2,1,0:T(8,128)S(1)} custom-call(f32[2,3,128,128]{3,2,1,0:T(8,128)} %ham_hbm.1, f32[2,3,128,128]{3,2,1,0:T(8,128)} %old_hbm.1, s32[2,3]{1,0:T(2,128)S(1)} %copy-done, s32[2]{0:T(128)S(1)} %copy-done.1, f32[1]{0:T(128)S(6)} %copy.7.pot_hbm), custom_call_target="tpu_custom_call" | custom-call | tf_op jit(solution)/shard_map/density/pallas_call | solution.py:377
  31.7 0.7 %copy.8 = f32[2,3,128,128]{3,2,1,0:T(8,128)} copy(f32[2,3,128,128]{3,2,1,0:T(8,128)S(1)} %density.1) | data formatting | bytes 786432
Async XLA Ops:
  0.0 0.7 %copy-start.1 = (s32[2]{0:T(128)S(1)}, s32[2]{0:T(128)}, u32[]{:S(2)}) copy-start(s32[2]{0:T(128)} %live_hbm.1) | copy-start | bytes 28
  0.0 0.7 %copy-start = (s32[2,3]{1,0:T(2,128)S(1)}, s32[2,3]{1,0:T(2,128)}, u32[]{:S(2)}) copy-start(s32[2,3]{1,0:T(2,128)} %nbr_hbm.1) | copy-start | bytes 76

commit v4 on v3

--- a/solution.py
+++ b/solution.py
@@ -139,10 +139,9 @@
         x, xh, xl, sh, sl = block(s)
         for i in range(3):
             for k in range(3):
-                rows, cols = tile(i), tile(k)
-                value = jnp.zeros((BLK, BLK), F32) if tiles[i][k] is None else tiles[i][k]
-                x[rows, cols] = value
-                put(xh, xl, rows, cols, value)
+                if tiles[i][k] is not None:
+                    x[tile(i), tile(k)] = tiles[i][k]
+                    put(xh, xl, tile(i), tile(k), tiles[i][k])
 
     def symmetric(left, right, first):
         def strip(ref, i, inner):
@@ -167,6 +166,8 @@
         for i, both in enumerate(symmetric((xh, xl), (xh, xl), first)):
             here, after = tile(i), tile((i + 1) % 3)
             own, side = both[:, 0:BLK], both[:, BLK : 2 * BLK]
+            if not first:
+                own, side = jnp.where(diagonal, 1.5, 0.0) - 0.5 * own, -0.5 * side
             put(sh, sl, here, here, own)
             put(sh, sl, here, after, side)
             put(sh, sl, after, here, side.T)
@@ -195,17 +196,20 @@
         put(sh, sl, FIRST, mine, side.T)
         put(sh, sl, mine, mine, base[s, 0] + more[:, BLK : 2 * BLK])
 
-    def advance(s, scale=None):
+    def advance(s, scale=None, final=False):
         x, xh, xl, sh, sl = block(s)
-        once, thrice = (1.5, 0.5) if scale is None else (1.5 * scale, 0.5 * scale * scale * scale)
         for i, both in enumerate(symmetric((xh, xl), (sh, sl), scale is not None)):
             here, after = tile(i), tile((i + 1) % 3)
-            own = once * x[here, here] - thrice * both[:, 0:BLK]
-            side = once * x[here, after] - thrice * both[:, BLK : 2 * BLK]
+            own, side = both[:, 0:BLK], both[:, BLK : 2 * BLK]
+            if scale is not None:
+                once, thrice = 1.5 * scale, 0.5 * scale * scale * scale
+                own = once * x[here, here] - thrice * own
+                side = once * x[here, after] - thrice * side
             turn = side.T
-            x[here, here] = own
-            x[here, after] = side
-            if i == 2:
+            if final and i == 0:
+                x[here, here] = own
+                x[here, after] = side
+            if final and i == 2:
                 x[after, here] = turn
             put(xh, xl, here, here, own)
             put(xh, xl, here, after, side)
@@ -220,12 +224,16 @@
     turned[0] = t1a_t
     turned[1] = t2b_t
     d_a, d_b = on_a - level, on_b - level
-    assemble(0, ((d_a, ham[a, 1], ham[a, 2]), (t1a_t, None, None), (ham[b, 1], None, d_b)))
-    assemble(1, ((d_b, ham[b, 1], ham[b, 2]), (ham[a, 2], d_a, None), (t2b_t, None, None)))
+    none, nil = (None, None, None), jnp.zeros((BLK, BLK), F32)
+    assemble(0, ((d_a, ham[a, 1], ham[a, 2]), (t1a_t, nil, nil), (ham[b, 1], nil, d_b)))
+    assemble(1, ((d_b, ham[b, 1], ham[b, 2]), (ham[a, 2], d_a, nil), (t2b_t, nil, nil)))
+    assemble(2, ((None, None, t1a_t), (None, None, nil), (ham[a, 1], nil, d_a)))
+    assemble(3, ((None, t2b_t, None), (ham[b, 2], d_b, nil), (None, nil, None)))
     square(0, True, 1)
     square(1, True, 2)
     most_a = jnp.maximum(sums(d_a, t1a_t, ham[b, 1]), sums(ham[a, 2], d_b))
     most_b = jnp.maximum(sums(d_b, ham[a, 2], t2b_t), sums(ham[b, 1], d_a))
+    most_prev, most_next = sums(t1a_t, d_a), sums(t2b_t, d_b)
     part_a, part_b = sums(ham[a, 1]), sums(ham[b, 2])
 
     wait_all(got_note, recv.at[0])
@@ -297,13 +305,16 @@
     d_prev, d_next = on_prev - level, on_next - level
     complete(0, 1, d_prev)
     complete(1, 2, d_next)
+    assemble(2, ((d_prev, None, None), none, none))
+    assemble(3, ((d_next, None, None), none, none))
+    part_prev, part_next = part_a + sums(d_prev), part_b + sums(d_next)
     advance(0, scale_of(jnp.maximum(most_a, part_a + sums(d_prev))))
     advance(1, scale_of(jnp.maximum(most_b, part_b + sums(d_next))))
     for sweep in range(ITERS - 2):
         square(0)
         square(1)
-        advance(0)
-        advance(1)
+        advance(0, final=sweep == ITERS - 3)
+        advance(1, final=sweep == ITERS - 3)
 
     new_a = finish(0, ALL)
     new_b = finish(1, ALL)
@@ -330,35 +341,36 @@
     out[1, 2] = f2b.T
 
     wait_all(far, recv.at[5])
-    wait_all(last, recv.at[6])
     on_prev_prev, on_next_next = unpack(far[:, 0:STRIP].reshape(BLK, BLK), diag_next)
     far_prev = far[:, STRIP : 2 * STRIP].reshape(BLK, BLK)
     far_prev_t = far_prev.T
-    d_prev_prev = on_prev_prev - level
-    on_next, on_prev = unpack(near[...].reshape(BLK, BLK), diag_prev)
-    d_prev, d_next, d_a, d_b = on_prev - level, on_next - level, on_a - level, on_b - level
-    assemble(2, ((d_prev, far_prev, turned[0]), (far_prev_t, d_prev_prev, None), (ham[a, 1], None, d_a)))
+    d_prev_prev, d_next_next = on_prev_prev - level, on_next_next - level
+    assemble(2, ((None, far_prev, None), (far_prev_t, d_prev_prev, None), none))
+    assemble(3, (none, none, (None, None, d_next_next)))
+    square(2, True)
+    base[0, 0] = far_prev_t
     scale_prev = scale_of(jnp.maximum(
-        jnp.maximum(sums(d_prev, far_prev_t, ham[a, 1]), sums(far_prev, d_prev_prev)), sums(turned[0], d_a)
+        jnp.maximum(part_prev + sums(far_prev_t), most_prev), sums(far_prev, d_prev_prev)
     ))
+    last_sums = sums(d_next_next)
+    wait_all(last, recv.at[6])
     far_next = last[...].reshape(BLK, BLK)
     far_next_t = far_next.T
-    d_next_next = on_next_next - level
-    assemble(3, ((d_next, turned[1], far_next), (ham[b, 2], d_b, None), (far_next_t, None, d_next_next)))
+    assemble(3, ((None, None, far_next), none, (far_next_t, None, None)))
+    square(3, True)
+    base[0, 1] = far_next_t
     scale_next = scale_of(jnp.maximum(
-        jnp.maximum(sums(d_next, ham[b, 2], far_next_t), sums(turned[1], d_b)), sums(far_next, d_next_next)
+        jnp.maximum(part_next + sums(far_next_t), most_next), sums(far_next) + last_sums
     ))
-    square(2, True)
-    square(3, True)
     advance(2, scale_prev)
     advance(3, scale_next)
     for sweep in range(ITERS - 2):
         square(2)
         square(3)
-        advance(2)
-        advance(3)
-    edge_prev = jnp.where(live_prev == 1.0, -0.5 * finish(2, tile(2)), far[:, STRIP : 2 * STRIP].reshape(BLK, BLK).T)
-    edge_next = jnp.where(live_next == 1.0, -0.5 * finish(3, tile(1)), last[...].reshape(BLK, BLK).T)
+        advance(2, final=sweep == ITERS - 3)
+        advance(3, final=sweep == ITERS - 3)
+    edge_prev = jnp.where(live_prev == 1.0, -0.5 * finish(2, tile(2)), base[0, 0])
+    edge_next = jnp.where(live_next == 1.0, -0.5 * finish(3, tile(1)), base[0, 1])
     outer_a = 0.5 * (out[0, 1] + edge_prev)
     outer_b = 0.5 * (out[1, 2] + edge_next)
     emit(1, outer_a, out[1, 1])

time: 32.6 us -> 32.7 us (level)
  no operation moved by 1% of the time
where the time goes in v4:
time: 32.7 us; the launch traced here: 32.5 us
  Pallas kernels  31.1 us (95%)
  local copies, waits for them, and re-layouts  0.76 us (2%)
  between operations  0.7 us (2%)
    pallas_call x1, Pallas kernels, shards(): pl.pallas_call(kernel, out_shape=jax.ShapeDtypeStruct((2, 3, BLK, BLK), F...  31.1 us
    unnamed x5, local copies, waits for them, and re-layouts  0.76 us

profile of v4, /device:TPU:1, one launch (start us, length us, event | category | flops | bytes accessed | tf_op | source)
XLA Modules:
  0.0 32.5 jit_solution(1460865625533380875)
XLA Ops:
  0.0 0.0 copy-start.1
  0.0 0.0 copy-start
  0.7 0.0 copy-done.1
  0.7 0.0 copy-done
  0.7 31.1 %density.1 = f32[2,3,128,128]{3,2,1,0:T(8,128)S(1)} custom-call(f32[2,3,128,128]{3,2,1,0:T(8,128)} %ham_hbm.1, f32[2,3,128,128]{3,2,1,0:T(8,128)} %old_hbm.1, s32[2,3]{1,0:T(2,128)S(1)} %copy-done, s32[2]{0:T(128)S(1)} %copy-done.1, f32[1]{0:T(128)S(6)} %copy.7.pot_hbm), custom_call_target="tpu_custom_call" | custom-call | tf_op jit(solution)/shard_map/density/pallas_call | solution.py:389
  31.8 0.7 %copy.8 = f32[2,3,128,128]{3,2,1,0:T(8,128)} copy(f32[2,3,128,128]{3,2,1,0:T(8,128)S(1)} %density.1) | data formatting | bytes 786432
Async XLA Ops:
  0.0 0.7 %copy-start.1 = (s32[2]{0:T(128)S(1)}, s32[2]{0:T(128)}, u32[]{:S(2)}) copy-start(s32[2]{0:T(128)} %live_hbm.1) | copy-start | bytes 28
  0.0 0.7 %copy-start = (s32[2,3]{1,0:T(2,128)S(1)}, s32[2,3]{1,0:T(2,128)}, u32[]{:S(2)}) copy-start(s32[2,3]{1,0:T(2,128)} %nbr_hbm.1) | copy-start | bytes 76

commit v5 on v4

--- a/solution.py
+++ b/solution.py
@@ -40,7 +40,7 @@
     ham_hbm, old_hbm, nbr_hbm, live_hbm, pot_hbm, out,
     ham, old, nbr, live, pot,
     packed, outer_next, outer_prev, note, got_packed, got_next, got_prev, got_note,
-    pick_near, pick_far, pick_last, near, far, last, turned, base,
+    pick_near, pick_onsite, pick_far, pick_last, near, onsite, far, last, turned, base,
     x_all, xh_all, xl_all, sh_all, sl_all,
     load, send, recv,
 ):
@@ -50,18 +50,22 @@
     def peer(j):
         return (w, (n + j) & (PEERS - 1))
 
+    barrier = pltpu.get_barrier_semaphore()
+
+    def far_first(m):
+        return PEERS // 2 + (1 - 2 * (m & 1)) * ((m + 1) >> 1)
+
+    def greet(m, _):
+        j = far_first(m)
+        pl.semaphore_signal(barrier, inc=1, device_id=peer(j), device_id_type=pl.DeviceIdType.MESH)
+        return _
+
+    lax.fori_loop(0, PEERS - 1, greet, 0)
+
     inputs = ((nbr_hbm, nbr), (ham_hbm, ham), (live_hbm, live), (old_hbm, old), (pot_hbm, pot))
     loads = [pltpu.make_async_copy(src, dst, load.at[i]) for i, (src, dst) in enumerate(inputs)]
     for copy in loads:
         copy.start()
-
-    barrier = pltpu.get_barrier_semaphore()
-
-    def greet(j, _):
-        pl.semaphore_signal(barrier, inc=1, device_id=peer(j), device_id_type=pl.DeviceIdType.MESH)
-        return _
-
-    lax.fori_loop(1, PEERS, greet, 0)
 
     for copy in loads:
         copy.wait()
@@ -103,7 +107,7 @@
 
     def to_all(*moves):
         def step(m, _):
-            j = PEERS // 2 + (1 - 2 * (m & 1)) * ((m + 1) >> 1)
+            j = far_first(m)
             for src, dst, which in moves:
                 push(src.at[0 if src is note else (n + j) & (PEERS - 1)], dst.at[j], which, j).start()
             return _
@@ -267,17 +271,24 @@
         push(pick_near.at[j], near.at[n], 4, j).start()
     near[n] = route_near(0)
 
+    def route_onsite(j):
+        to_prev, to_next = offsets(j)
+        return select(j, jnp.where(below, to_next, to_prev), lambda k: got_packed[k])
+
+    for j in ORDER_OUT:
+        pick_onsite[j] = route_onsite(j)
+        push(pick_onsite.at[j], onsite.at[n], 7, j).start()
+    onsite[n] = route_onsite(0)
+
     wait_all(got_next, recv.at[2])
 
-    def route_far(j, ref):
-        to_prev, to_next = offsets(j)
-        ref[0:STRIP] = select(j, jnp.where(below, to_next, to_prev), lambda k: got_packed[k])
-        ref[STRIP : 2 * STRIP] = select(j, to_prev, lambda k: got_next[k])
+    def route_far(j):
+        return select(j, offsets(j)[0], lambda k: got_next[k])
 
     for j in ORDER_OUT:
-        route_far(j, pick_far.at[j])
+        pick_far[j] = route_far(j)
         push(pick_far.at[j], far.at[n], 5, j).start()
-    route_far(0, far.at[n])
+    far[n] = route_far(0)
 
     wait_all(got_prev, recv.at[3])
 
@@ -340,19 +351,22 @@
     out[0, 2] = inner
     out[1, 2] = f2b.T
 
+    wait_all(onsite, recv.at[7])
+    on_prev_prev, on_next_next = unpack(onsite[...].reshape(BLK, BLK), diag_next)
+    d_prev_prev, d_next_next = on_prev_prev - level, on_next_next - level
+    assemble(2, (none, (None, d_prev_prev, None), none))
+    assemble(3, (none, none, (None, None, d_next_next)))
+    first_sums, last_sums = sums(d_prev_prev), sums(d_next_next)
+
     wait_all(far, recv.at[5])
-    on_prev_prev, on_next_next = unpack(far[:, 0:STRIP].reshape(BLK, BLK), diag_next)
-    far_prev = far[:, STRIP : 2 * STRIP].reshape(BLK, BLK)
+    far_prev = far[...].reshape(BLK, BLK)
     far_prev_t = far_prev.T
-    d_prev_prev, d_next_next = on_prev_prev - level, on_next_next - level
-    assemble(2, ((None, far_prev, None), (far_prev_t, d_prev_prev, None), none))
-    assemble(3, (none, none, (None, None, d_next_next)))
+    assemble(2, ((None, far_prev, None), (far_prev_t, None, None), none))
     square(2, True)
     base[0, 0] = far_prev_t
     scale_prev = scale_of(jnp.maximum(
-        jnp.maximum(part_prev + sums(far_prev_t), most_prev), sums(far_prev, d_prev_prev)
+        jnp.maximum(part_prev + sums(far_prev_t), most_prev), sums(far_prev) + first_sums
     ))
-    last_sums = sums(d_next_next)
     wait_all(last, recv.at[6])
     far_next = last[...].reshape(BLK, BLK)
     far_next_t = far_next.T
@@ -376,14 +390,13 @@
     emit(1, outer_a, out[1, 1])
     emit(2, out[0, 2], outer_b)
 
-    for i, ref in enumerate((got_note, got_packed, got_next, got_prev, near, far, last)):
+    for i, ref in enumerate((got_note, got_packed, got_next, got_prev, near, far, last, onsite)):
         wait_all(ref, send.at[i])
 
 
 def shards(hamiltonian, old_density, neighbours, live, potential):
     hbm = pl.BlockSpec(memory_space=pltpu.HBM)
     strips = pltpu.VMEM((PEERS, STRIP, BLK), F32)
-    two_strips = pltpu.VMEM((PEERS, 2 * STRIP, BLK), F32)
     matrices = pltpu.VMEM((4, ORDER, ORDER), F32)
     matrix_halves = pltpu.VMEM((4, ORDER, ORDER), BF16)
     return pl.pallas_call(
@@ -399,13 +412,13 @@
             pltpu.SMEM((1,), F32),
             strips, strips, strips, pltpu.VMEM((1, 1, 2 * BLK), F32),
             strips, strips, strips, pltpu.VMEM((PEERS, 1, 2 * BLK), F32),
-            strips, two_strips, strips, strips, two_strips, strips,
+            strips, strips, strips, strips, strips, strips, strips, strips,
             pltpu.VMEM((2, BLK, BLK), F32),
             pltpu.VMEM((2, 2, BLK, BLK), F32),
             matrices, matrix_halves, matrix_halves, matrix_halves, matrix_halves,
             pltpu.SemaphoreType.DMA((5,)),
-            pltpu.SemaphoreType.DMA((7,)),
-            pltpu.SemaphoreType.DMA((7,)),
+            pltpu.SemaphoreType.DMA((8,)),
+            pltpu.SemaphoreType.DMA((8,)),
         ],
         compiler_params=pltpu.CompilerParams(
             collective_id=0, has_side_effects=True, vmem_limit_bytes=VMEM_LIMIT

time: 32.7 us -> 33 us (level)
    pallas_call x1, Pallas kernels: 31.1 us -> 31.4 us  [shards(): pl.pallas_call(kernel, out_shape=jax.ShapeDtypeStruct((2, 3, BLK, BLK), F...]
where the time goes in v5:
time: 33 us; the launch traced here: 32.9 us
  Pallas kernels  31.4 us (95%)
  local copies, waits for them, and re-layouts  0.76 us (2%)
  between operations  0.7 us (2%)
    pallas_call x1, Pallas kernels, shards(): pl.pallas_call(kernel, out_shape=jax.ShapeDtypeStruct((2, 3, BLK, BLK), F...  31.4 us
    unnamed x5, local copies, waits for them, and re-layouts  0.76 us

profile of v5, /device:TPU:1, one launch (start us, length us, event | category | flops | bytes accessed | tf_op | source)
XLA Modules:
  0.0 32.9 jit_solution(18007828611454633005)
XLA Ops:
  0.0 0.0 copy-start.1
  0.0 0.0 copy-start
  0.7 0.0 copy-done.1
  0.7 0.0 copy-done
  0.7 31.4 %density.1 = f32[2,3,128,128]{3,2,1,0:T(8,128)S(1)} custom-call(f32[2,3,128,128]{3,2,1,0:T(8,128)} %ham_hbm.1, f32[2,3,128,128]{3,2,1,0:T(8,128)} %old_hbm.1, s32[2,3]{1,0:T(2,128)S(1)} %copy-done, s32[2]{0:T(128)S(1)} %copy-done.1, f32[1]{0:T(128)S(6)} %copy.7.pot_hbm), custom_call_target="tpu_custom_call" | custom-call | tf_op jit(solution)/shard_map/density/pallas_call | solution.py:402
  32.1 0.7 %copy.8 = f32[2,3,128,128]{3,2,1,0:T(8,128)} copy(f32[2,3,128,128]{3,2,1,0:T(8,128)S(1)} %density.1) | data formatting | bytes 786432
Async XLA Ops:
  0.0 0.7 %copy-start.1 = (s32[2]{0:T(128)S(1)}, s32[2]{0:T(128)}, u32[]{:S(2)}) copy-start(s32[2]{0:T(128)} %live_hbm.1) | copy-start | bytes 28
  0.0 0.7 %copy-start = (s32[2,3]{1,0:T(2,128)S(1)}, s32[2,3]{1,0:T(2,128)}, u32[]{:S(2)}) copy-start(s32[2,3]{1,0:T(2,128)} %nbr_hbm.1) | copy-start | bytes 76
